TPU v7x, 32 devices: a whole 2x2x4 slice. The times are simulated.
32 devices in a mesh: groups: 2 (over y), sub: 8 (over z, x), sector: 2 (over core).
Axes of the slice: x: 2, y: 2, z: 4, core: 2. Of those that a mesh axis runs over, the one named last changes fastest.
Arguments:
- ingest: bfloat16 [128, 128, 512], P(('groups', 'sub')), parts along dimension 0, may hold values from -6 to 6
- replica: bfloat16 [2, 512], replicated, may hold values from -0.1875 to 0.1875
- counts: int32 [16], P(('groups', 'sub')), parts along dimension 0, may hold values from 1 to 7, as said below
- track_list: int32 [128], P(('groups', 'sub')), parts along dimension 0, may hold values from -1 to 6, as said below
- deviation: float32 [64], P(('groups', 'sub')), parts along dimension 0, may hold values from -3 to 3
- offsets: int32 [3, 2, 16, 8], P(None, None, ('groups', 'sub'), 'sector'), parts along dimension 2, may hold values from -64 to 64
- fraction: float32 [3, 2, 16, 8], P(None, None, ('groups', 'sub'), 'sector'), parts along dimension 2, may hold values from 0 to 1
Outputs:
- polar_image: bfloat16 [2, 16, 8, 32768], P(None, ('groups', 'sub'), 'sector'), parts along dimension 1
There are 2 independent parts, one for each index of `groups`. A program takes and returns all parts, laid end to end along the dimension named above; an argument that names none is the same for every part. Nothing has to cross between parts.
Inputs may be any that keep to these rules, and one draw needn't show every extreme that they name: Owner a ingests the pulses numbered starts[a] to starts[a] + counts[a] - 1, with starts[a] = counts[0] + ... + counts[a - 1] between a * 4 and a * 4 + 3; the counts sum to 32; in every draw some owner holds 3 pulses of the next owner's subaperture. `track_list`: on owner a, exactly counts[a] of its 8 slots hold the numbers 0 to counts[a] - 1, each once; the other slots hold -1.
All inputs are finite; a program needn't handle non-finite values.
Results may differ from a plain program's by a relative error of at most 0.014.
Values may be sent and summed in bfloat16 or wider, within the bound.
A program may use at most 64 MiB of HBM per device.

v0:
```python
import math

import jax
import jax.numpy as jnp
from jax import lax
from jax.sharding import PartitionSpec as P

SECTIONS = 3


BIN_WAVES = 0.85
TILE_BINS = 128


def prefix(value, axis, join, neutral):
    count, mine = (lax.axis_size(axis), lax.axis_index(axis))
    pieces = lax.all_gather(value, axis)
    total = jnp.full_like(value, 0) + jnp.asarray(neutral, value.dtype)

    def lap(position, total):
        longer = join(total, pieces[position])
        return jnp.where(position < mine, longer, total)

    return lax.fori_loop(0, count - 1, lap, total)


def from_behind(block, axis, distance):
    devices = range(lax.axis_size(axis))
    route = [(i - distance, i) for i in devices if i - distance in devices]
    return lax.ppermute(block, axis, route)


def partner_2(block, axis, apart):
    count = lax.axis_size(axis)
    route = []
    for low in range(count):
        high = low | 1 << apart
        if high != low and high < count:
            route += [(low, high), (high, low)]
    return lax.ppermute(block, axis, route)


def filter_blocks(replica, segment):
    taps_count = replica.shape[1]
    window = segment + taps_count
    response = replica.astype(jnp.float32)
    pattern = jnp.concatenate([response, jnp.zeros((2, segment + 1), jnp.float32)], axis=1)
    skewed = jnp.tile(pattern, (1, segment))[:, : segment * window].reshape(2, segment, window)
    banded = jnp.transpose(skewed, (0, 2, 1))
    upper_rows = jnp.concatenate([banded[0], -banded[1]], axis=1)
    lower_rows = jnp.concatenate([banded[1], banded[0]], axis=1)
    matrices = []
    for block_index in range(window // segment):
        first_row = block_index * segment
        matrices.append(
            jnp.concatenate(
                [
                    upper_rows[first_row : first_row + segment],
                    lower_rows[first_row : first_row + segment],
                ],
                axis=0,
            )
        )
    return jnp.stack(matrices).astype(jnp.bfloat16)


def compress_rows(pulse_rows, filters):
    filter_count = filters.shape[0]
    blocks_count = pulse_rows.shape[1]
    padded = jnp.pad(pulse_rows, ((0, 0), (0, filter_count - 1), (0, 0)))
    result = jnp.zeros(pulse_rows.shape, jnp.float32)
    for block_index in range(filter_count):
        result = result + jnp.einsum(
            "rkc,cd->rkd",
            padded[:, block_index : block_index + blocks_count],
            filters[block_index],
            preferred_element_type=jnp.float32,
        )
    return result.astype(jnp.bfloat16)


def cubic_weights(fractions):
    square = fractions * fractions
    cubed = square * fractions
    return (
        -0.5 * cubed + square - 0.5 * fractions,
        1.5 * cubed - 2.5 * square + 1.0,
        -1.5 * cubed + 2.0 * square + 0.5 * fractions,
        0.5 * cubed - 0.5 * square,
    )


def interpolate(child, shifts, fractions):
    parts_count, beams, length = child.shape
    blocks = length // TILE_BINS
    padded = jnp.pad(child, ((0, 0), (0, 0), (TILE_BINS, TILE_BINS))).reshape(
        parts_count, beams, blocks + 2, TILE_BINS
    )
    window = jnp.concatenate(
        [padded[:, :, 0:blocks], padded[:, :, 1 : blocks + 1], padded[:, :, 2 : blocks + 2]], axis=3
    )
    weights = cubic_weights(fractions)
    rows_at = jnp.arange(3 * TILE_BINS, dtype=jnp.int32)[:, None]
    cols_at = jnp.arange(TILE_BINS, dtype=jnp.int32)[None, :]
    distance = (rows_at - cols_at - TILE_BINS)[None, :, :] - shifts[:, None, None]
    band = jnp.zeros((beams, 3 * TILE_BINS, TILE_BINS), jnp.float32)
    for tap_index in range(4):
        band = band + jnp.where(distance == tap_index - 1, weights[tap_index][:, None, None], 0.0)
    band_high = band.astype(jnp.bfloat16)
    band_low = (band - band_high.astype(jnp.float32)).astype(jnp.bfloat16)
    summed = jnp.einsum("pbkj,bjn->pbkn", window, band_high, preferred_element_type=jnp.float32)
    summed = summed + jnp.einsum(
        "pbkj,bjn->pbkn", window, band_low, preferred_element_type=jnp.float32
    )
    summed = summed.reshape(parts_count, beams, length)
    rotation = 2.0 * math.pi * BIN_WAVES * (shifts.astype(jnp.float32) + fractions)
    cosine = jnp.cos(rotation)[:, None]
    sine_part = jnp.sin(rotation)[:, None]
    return jnp.stack(
        [cosine * summed[0] - sine_part * summed[1], sine_part * summed[0] + cosine * summed[1]]
    )


def merge_pair(lower_image, upper_image, shifts, fractions):
    combined = interpolate(lower_image, shifts[0], fractions[0]) + interpolate(
        upper_image, shifts[1], fractions[1]
    )
    return (combined * (1.0 / math.sqrt(2.0))).astype(jnp.bfloat16)


def on_device(ingest, replica, counts, track_list, deviation, offsets, fraction):
    pulses = ingest.shape[0] // 2
    blocks_count = ingest.shape[1]
    segment = ingest.shape[2] // 2
    samples = blocks_count * segment
    owner_index = lax.axis_index("sub")
    start_here = prefix(
        counts, "sub", lambda earlier, later: earlier + later, jnp.zeros_like(counts)
    )[0]
    filters = filter_blocks(replica, segment)
    slot_rows = compress_rows(ingest, filters)
    position_in_run = start_here - owner_index * pulses + track_list
    targets = jnp.arange(2 * pulses, dtype=jnp.int32)
    selector = ((position_in_run[None, :] == targets[:, None]) & (track_list[None, :] >= 0)).astype(
        jnp.bfloat16
    )
    routed = jnp.einsum(
        "qs,skc->qkc", selector, slot_rows, preferred_element_type=jnp.float32
    ).astype(jnp.bfloat16)
    received = from_behind(routed[pulses:], "sub", 1)
    owned = routed[:pulses] + received
    beams_total = lax.axis_size("sector") * pulses
    beam_index = (lax.axis_index("sector") * pulses + jnp.arange(pulses)).astype(jnp.float32)
    beam_angle = (beam_index + 0.5) / beams_total - 0.5
    pulse_index = jnp.arange(pulses).astype(jnp.float32)
    position = 2.0 * (pulse_index - (pulses - 1) / 2.0) + deviation
    phase_angle = 2.0 * math.pi * position[None, :] * beam_angle[:, None]
    scale = 1.0 / math.sqrt(pulses)
    real_weight = (jnp.cos(phase_angle) * scale).astype(jnp.bfloat16)
    imag_weight = (jnp.sin(phase_angle) * scale).astype(jnp.bfloat16)
    stacked = jnp.stack(
        [jnp.stack([real_weight, -imag_weight]), jnp.stack([imag_weight, real_weight])]
    )
    spread = owned.reshape(pulses, blocks_count, 2, segment)
    images = jnp.einsum("oibp,pkis->obks", stacked, spread, preferred_element_type=jnp.float32)
    images = images.astype(jnp.bfloat16).reshape(2, pulses, samples)
    for section_index in range(SECTIONS):
        partner = partner_2(images, "sub", section_index)
        upper_side = owner_index >> section_index & 1 == 1
        lower_image = jnp.where(upper_side, partner, images)
        upper_image = jnp.where(upper_side, images, partner)
        images = merge_pair(
            lower_image, upper_image, offsets[section_index, :, 0], fraction[section_index, :, 0]
        )
    return images.reshape(2, 1, pulses, samples)


def solution(mesh):
    return jax.shard_map(
        on_device,
        mesh=mesh,
        in_specs=(
            P(("groups", "sub"), None, None),
            P(),
            P(("groups", "sub")),
            P(("groups", "sub")),
            P(("groups", "sub")),
            P(None, None, ("groups", "sub"), "sector"),
            P(None, None, ("groups", "sub"), "sector"),
        ),
        out_specs=P(None, ("groups", "sub"), "sector", None),
        check_vma=False,
    )
```

profile of v0, /device:TPU:0, one launch (start us, length us, event | category | flops | bytes accessed | tf_op | source)
XLA Modules:
  0.0 127.3 jit_solution(5978822957109547863)
XLA Ops:
  0.0 0.7 pad_convert_fusion
  0.8 2.2 %tile.10 = f32[2,196864]{1,0:T(2,128)S(1)} reshape(f32[2,256,769]{2,1,0:T(8,128)S(1)} %tile.4) | data formatting | bytes 3149824 | tf_op jit(solution)/shard_map/tile | solution.py:48
  3.5 1.1 copy-done
  4.6 1.5 %pad_slice_fusion = (bf16[8,128,512]{2,1,0:T(8,128)(2,1)}, bf16[8,128,512]{2,1,0:T(8,128)(2,1)S(1)}) fusion(bf16[8,128,512]{2,1,0:T(8,128)(2,1)S(1)} %copy-done), kind=kLoop, calls=%fused_computation.78 | loop fusion | bytes 3145728 | tf_op jit(solution)/shard_map/slice | solution.py:75
  6.7 0.6 dynamic-slice
  7.3 0.7 dynamic-update-slice
  8.0 13.1 %all-reduce.8 = s32[8]{0:T(128)S(1)} all-reduce(s32[8]{0:T(128)S(1)} %dynamic-update-slice), channel_id=2, replica_groups=mesh['groups'=2,'sub'=8,'sector'=2] {'sub'}, use_global_device_ids=true, to_apply=%add.8 | all-reduce | flops 8 | bytes 64
  21.1 9.0 %while.13 = (s32[]{:T(128)}, s32[1]{0:T(128)}, s32[]{:T(128)}, s32[8,1]{0,1:T(1,128)S(1)}, s32[]{:T(128)}) while((s32[]{:T(128)}, s32[1]{0:T(128)}, s32[]{:T(128)}, s32[8,1]{0,1:T(1,128)S(1)}, s32[]{:T(128)}) %tuple.112), condition=%wide.region_1.2_spmd, body=%wide.region_0.1_spmd.sunk | while | flops 5 | bytes 107 | solution.py:24
  21.1 0.6 constant_dynamic-slice_fusion.2
  22.4 0.6 constant_dynamic-slice_fusion.2
  23.7 0.6 constant_dynamic-slice_fusion.2
  25.0 0.6 constant_dynamic-slice_fusion.2
  26.2 0.6 constant_dynamic-slice_fusion.2
  27.5 0.6 constant_dynamic-slice_fusion.2
  28.8 0.6 constant_dynamic-slice_fusion.2
  30.2 0.8 fusion.263
  31.0 2.1 %fusion.37 = f32[512,8,128]{0,1,2:T(8,128)} fusion(bf16[8,128,512]{2,1,0:T(8,128)(2,1)S(1)} %copy-done, bf16[256,512]{0,1:T(8,128)(2,1)S(1)} %get-tuple-element.202, bf16[256,512]{0,1:T(8,128)(2,1)S(1)} %get-tuple-element.129), kind=kOutput, calls=%fused_computation.72 | convolution fusion | flops 537919488 | bytes 3670016 | tf_op jit(solution)/shard_map/rkc,cd->rkd/dot_general | solution.py:73
  33.2 0.8 fusion.35
  34.0 3.1 %convolution_convert_fusion = bf16[8,128,512]{2,0,1:T(8,128)(2,1)S(1)} fusion(f32[8,128,512]{2,0,1:T(8,128)S(1)} %fusion.35, f32[512,8,128]{0,1,2:T(8,128)} %fusion.37, bf16[8,128,512]{2,1,0:T(8,128)(2,1)} %get-tuple-element.125, bf16[256,512]{0,1:T(8,128)(2,1)} %get-tuple-element.204, bf16[256,512]{0,1:T(8,128)(2,1)S(1)} %get-tuple-element.127, ...), kind=kOutput, calls=%fused_computation.37 | convolution fusion | flops 548405376 | bytes 6815784 | tf_op jit(solution)/shard_map/qs,skc->qkc/dot_general | solution.py:147
  37.4 3.6 %collective-permute-start = (bf16[4,128,512]{2,0,1:T(4,128)(2,1)S(1)}, bf16[4,128,512]{2,0,1:T(4,128)(2,1)S(1)}, u32[]{:S(2)}, u32[]{:S(2)}) collective-permute-start(bf16[4,128,512]{2,0,1:T(4,128)(2,1)S(1)} %slice.296), channel_id=1, source_target_pairs={{0,2},{2,4},{4,6},{6,8},{8,10},{10,12},{12,14},{1,3},{3,5},{5,7},{... | collective-permute-start | bytes 1572872 | tf_op jit(solution)/shard_map/ppermute | solution.py:30
  41.3 8.2 %collective-permute-done = bf16[4,128,512]{2,0,1:T(4,128)(2,1)S(1)} collective-permute-done((bf16[4,128,512]{2,0,1:T(4,128)(2,1)S(1)}, bf16[4,128,512]{2,0,1:T(4,128)(2,1)S(1)}, u32[]{:S(2)}, u32[]{:S(2)}) %collective-permute-start) | collective-permute-done | bytes 524320 | tf_op jit(solution)/shard_map/ppermute | solution.py:30
  49.8 0.6 fusion.26
  50.4 2.5 %collective-permute-start.1 = (bf16[2,4,32768]{2,1,0:T(4,128)(2,1)S(1)}, bf16[2,4,32768]{2,1,0:T(4,128)(2,1)S(1)}, u32[]{:S(2)}, u32[]{:S(2)}) collective-permute-start(bf16[2,4,32768]{2,1,0:T(4,128)(2,1)S(1)} %bitcast.403), channel_id=1, source_target_pairs={{0,2},{2,0},{4,6},{6,4},{8,10},{10,8},{12,14},{14,12},{1,3},{3,1},... | collective-permute-start | bytes 1572872 | tf_op jit(solution)/shard_map/ppermute | solution.py:40
  53.1 7.5 %collective-permute-done.1 = bf16[2,4,32768]{2,1,0:T(4,128)(2,1)S(1)} collective-permute-done((bf16[2,4,32768]{2,1,0:T(4,128)(2,1)S(1)}, bf16[2,4,32768]{2,1,0:T(4,128)(2,1)S(1)}, u32[]{:S(2)}, u32[]{:S(2)}) %collective-permute-start.1) | collective-permute-done | bytes 524320 | tf_op jit(solution)/shard_map/ppermute | solution.py:40
  61.1 0.3 fusion.269
  61.4 0.7 fusion.2
  62.1 0.7 fusion.19
  64.1 0.7 fusion.6
  64.8 0.7 fusion.13
  66.0 1.0 multiply_subtract_fusion.2
  67.0 1.0 multiply_subtract_fusion.3
  67.9 2.2 %fusion.28 = bf16[2,4,32768]{2,0,1:T(2,128)(2,1)S(1)} fusion(f32[1,4,32768]{2,0,1:T(1,128)S(1)} %get-tuple-element.106, f32[1,4,32768]{2,0,1:T(1,128)S(1)} %get-tuple-element.105, f32[1,4,32768]{2,0,1:T(1,128)S(1)} %get-tuple-element.104, f32[1,4,32768]{2,0,1:T(1,128)S(1)} %get-tuple-element.103), kind=kLoop, calls=%fused_computation.62 | loop fusion | flops 1310720 | bytes 2621440 | tf_op jit(solution)/shard_map/convert_element_type | solution.py:128
  70.1 2.4 %collective-permute-start.2 = (bf16[2,4,32768]{2,0,1:T(2,128)(2,1)S(1)}, bf16[2,4,32768]{2,0,1:T(2,128)(2,1)S(1)}, u32[]{:S(2)}, u32[]{:S(2)}) collective-permute-start(bf16[2,4,32768]{2,0,1:T(2,128)(2,1)S(1)} %fusion.28), channel_id=1, source_target_pairs={{0,4},{4,0},{2,6},{6,2},{8,12},{12,8},{10,14},{14,10},{1,5},{5,1},... | collective-permute-start | bytes 1572872 | tf_op jit(solution)/shard_map/ppermute | solution.py:40
  72.6 7.6 %collective-permute-done.2 = bf16[2,4,32768]{2,0,1:T(2,128)(2,1)S(1)} collective-permute-done((bf16[2,4,32768]{2,0,1:T(2,128)(2,1)S(1)}, bf16[2,4,32768]{2,0,1:T(2,128)(2,1)S(1)}, u32[]{:S(2)}, u32[]{:S(2)}) %collective-permute-start.2) | collective-permute-done | bytes 524320 | tf_op jit(solution)/shard_map/ppermute | solution.py:40
  80.2 2.4 %broadcast_select_fusion = (bf16[2,4,32768]{2,0,1:T(2,128)(2,1)S(1)}, bf16[2,4,32768]{2,0,1:T(2,128)(2,1)S(1)}) fusion(bf16[2,4,32768]{2,0,1:T(2,128)(2,1)S(1)} %collective-permute-done.2, pred[]{:T(512)S(6)} %eq.103, f32[1,4,32768]{2,0,1:T(1,128)S(1)} %get-tuple-element.104, f32[1,4,32768]{2,0,1:T(1,128)S(1)} %get-tuple-element.103, ...), kind=kLoop, calls=%fused_computation.74 | loop fusion | flops 1835008 | bytes 3670017 | tf_op jit(solution)/shard_map/jit(_where)/select_n | solution.py:171
  82.6 0.4 pad.29
  83.0 0.3 reshape.1550
  83.4 0.3 fusion.267
  83.7 0.7 fusion.41
  84.4 0.7 fusion.24
  85.6 0.4 pad.28
  86.0 0.3 reshape.1549
  86.7 0.7 fusion.42
  87.4 0.7 fusion.25
  88.6 1.0 multiply_subtract_fusion
  89.6 1.0 multiply_subtract_fusion.1
  90.6 1.9 %fusion.30 = bf16[2,4,32768]{2,0,1:T(2,128)(2,1)S(1)} fusion(f32[1,4,32768]{2,0,1:T(1,128)S(1)} %get-tuple-element.102, f32[1,4,32768]{2,0,1:T(1,128)S(1)} %get-tuple-element.101, f32[1,4,32768]{2,0,1:T(1,128)S(1)} %get-tuple-element.100, f32[1,4,32768]{2,0,1:T(1,128)S(1)} %get-tuple-element.99), kind=kLoop, calls=%fused_computation.65 | loop fusion | flops 1310720 | bytes 2621440 | tf_op jit(solution)/shard_map/convert_element_type | solution.py:128
  92.6 1.6 %collective-permute-start.3 = (bf16[2,4,32768]{2,0,1:T(2,128)(2,1)S(1)}, bf16[2,4,32768]{2,0,1:T(2,128)(2,1)S(1)}, u32[]{:S(2)}, u32[]{:S(2)}) collective-permute-start(bf16[2,4,32768]{2,0,1:T(2,128)(2,1)S(1)} %fusion.30), channel_id=1, source_target_pairs={{0,8},{8,0},{2,10},{10,2},{4,12},{12,4},{6,14},{14,6},{1,9},{9,1},... | collective-permute-start | bytes 1572872 | tf_op jit(solution)/shard_map/ppermute | solution.py:40
  94.1 19.4 %collective-permute-done.3 = bf16[2,4,32768]{2,0,1:T(2,128)(2,1)S(1)} collective-permute-done((bf16[2,4,32768]{2,0,1:T(2,128)(2,1)S(1)}, bf16[2,4,32768]{2,0,1:T(2,128)(2,1)S(1)}, u32[]{:S(2)}, u32[]{:S(2)}) %collective-permute-start.3) | collective-permute-done | bytes 524320 | tf_op jit(solution)/shard_map/ppermute | solution.py:40
  113.5 2.7 %broadcast_select_fusion.2 = (bf16[2,4,32768]{2,0,1:T(2,128)(2,1)S(1)}, bf16[2,4,32768]{2,0,1:T(2,128)(2,1)S(1)}) fusion(bf16[2,4,32768]{2,0,1:T(2,128)(2,1)S(1)} %collective-permute-done.3, pred[]{:T(512)S(6)} %eq.98, f32[1,4,32768]{2,0,1:T(1,128)S(1)} %get-tuple-element.100, f32[1,4,32768]{2,0,1:T(1,128)S(1)} %get-tuple-element.99, ...), kind=kLoop, calls=%fused_computation.76 | loop fusion | flops 1835008 | bytes 3670017 | tf_op jit(solution)/shard_map/jit(_where)/select_n | solution.py:171
  116.2 0.4 pad.31
  116.6 0.3 reshape.1552
  117.0 0.3 fusion.265
  117.3 0.7 fusion.39
  118.0 0.7 fusion.22
  119.2 0.4 pad.30
  119.6 0.3 reshape.1551
  119.9 0.3 fusion.266
  120.3 0.7 fusion.40
  121.0 0.7 fusion.23
  122.2 1.0 subtract_bitcast_fusion
  123.2 1.0 subtract_bitcast_fusion.1
  124.2 1.9 %fusion.32 = bf16[2,1,4,32768]{3,0,2,1:T(2,128)(2,1)S(1)} fusion(f32[1,1,4,32768]{3,0,2,1:T(1,128)S(1)} %get-tuple-element.98, f32[1,1,4,32768]{3,0,2,1:T(1,128)S(1)} %get-tuple-element.97, f32[1,1,4,32768]{3,0,2,1:T(1,128)S(1)} %get-tuple-element.96, f32[1,1,4,32768]{3,0,2,1:T(1,128)S(1)} %get-tuple-element.95), kind=kLoop, calls=%fused_computation.68 | loop fusion | flops 1310720 | bytes 2621440 | tf_op jit(solution)/shard_map/convert_element_type | solution.py:128
  126.1 1.2 copy.44
  (56 shorter events, 5.9 us)
Async XLA Ops:
  3.3 1.2 copy-start
  4.6 2.1 %copy-start.5 = (u32[32]{0:T(128)S(1)}, u32[32]{0:T(128)}, u32[]{:S(2)}) copy-start(u32[32]{0:T(128)} %constant.105) | copy-start | bytes 388
  4.6 25.5 %copy-start.4 = (s32[8]{0:T(128)S(1)}, s32[8]{0:T(128)}, u32[]{:S(2)}) copy-start(s32[8]{0:T(128)} %param.12) | copy-start | bytes 100
  34.0 7.1 %copy-start.3 = (f32[4]{0:T(128)S(1)}, f32[4]{0:T(128)}, u32[]{:S(2)}) copy-start(f32[4]{0:T(128)} %param.13) | copy-start | bytes 52
  34.0 7.3 %copy-start.2 = (s32[3,2,1,4]{3,2,1,0:T(1,128)S(1)}, s32[3,2,1,4]{3,2,1,0:T(1,128)}, u32[]{:S(2)}) copy-start(s32[3,2,1,4]{3,2,1,0:T(1,128)} %param.14) | copy-start | bytes 292
  37.4 15.5 %copy-start.1 = (f32[3,2,1,4]{3,2,1,0:T(1,128)S(1)}, f32[3,2,1,4]{3,2,1,0:T(1,128)}, u32[]{:S(2)}) copy-start(f32[3,2,1,4]{3,2,1,0:T(1,128)} %param.15) | copy-start | bytes 292
  37.4 12.1 %collective-permute-start = (bf16[4,128,512]{2,0,1:T(4,128)(2,1)S(1)}, bf16[4,128,512]{2,0,1:T(4,128)(2,1)S(1)}, u32[]{:S(2)}, u32[]{:S(2)}) collective-permute-start(bf16[4,128,512]{2,0,1:T(4,128)(2,1)S(1)} %slice.296), channel_id=1, source_target_pairs={{0,2},{2,4},{4,6},{6,8},{8,10},{10,12},{12,14},{1,3},{3,5},{5,7},{... | collective-permute-start | bytes 1572872 | tf_op jit(solution)/shard_map/ppermute | solution.py:30
  50.4 10.2 %collective-permute-start.1 = (bf16[2,4,32768]{2,1,0:T(4,128)(2,1)S(1)}, bf16[2,4,32768]{2,1,0:T(4,128)(2,1)S(1)}, u32[]{:S(2)}, u32[]{:S(2)}) collective-permute-start(bf16[2,4,32768]{2,1,0:T(4,128)(2,1)S(1)} %bitcast.403), channel_id=1, source_target_pairs={{0,2},{2,0},{4,6},{6,4},{8,10},{10,8},{12,14},{14,12},{1,3},{3,1},... | collective-permute-start | bytes 1572872 | tf_op jit(solution)/shard_map/ppermute | solution.py:40
  70.1 10.1 %collective-permute-start.2 = (bf16[2,4,32768]{2,0,1:T(2,128)(2,1)S(1)}, bf16[2,4,32768]{2,0,1:T(2,128)(2,1)S(1)}, u32[]{:S(2)}, u32[]{:S(2)}) collective-permute-start(bf16[2,4,32768]{2,0,1:T(2,128)(2,1)S(1)} %fusion.28), channel_id=1, source_target_pairs={{0,4},{4,0},{2,6},{6,2},{8,12},{12,8},{10,14},{14,10},{1,5},{5,1},... | collective-permute-start | bytes 1572872 | tf_op jit(solution)/shard_map/ppermute | solution.py:40
  92.6 21.0 %collective-permute-start.3 = (bf16[2,4,32768]{2,0,1:T(2,128)(2,1)S(1)}, bf16[2,4,32768]{2,0,1:T(2,128)(2,1)S(1)}, u32[]{:S(2)}, u32[]{:S(2)}) collective-permute-start(bf16[2,4,32768]{2,0,1:T(2,128)(2,1)S(1)} %fusion.30), channel_id=1, source_target_pairs={{0,8},{8,0},{2,10},{10,2},{4,12},{12,4},{6,14},{14,6},{1,9},{9,1},... | collective-permute-start | bytes 1572872 | tf_op jit(solution)/shard_map/ppermute | solution.py:40
where the time goes:
time: 128 us; the launch traced here: 127 us
  waiting for transfers between devices  42.7 us (33%)
  local copies, waits for them, and re-layouts  21.9 us (17%)
  other arithmetic  18.7 us (15%)
  matrix products  15 us (12%)
  blocking collectives  13.1 us (10%)
  starting transfers between devices  10.1 us (8%)
  loops' own time  4.51 us (4%)
  between operations  1.32 us (1%)
    ppermute x3, waiting for transfers between devices, partner_2(): return lax.ppermute(block, axis, route)  34.5 us
    unnamed x1, blocking collectives  13.1 us
    ppermute x1, waiting for transfers between devices, from_behind(): return lax.ppermute(block, axis, route)  8.19 us
    ppermute x3, starting transfers between devices, partner_2(): return lax.ppermute(block, axis, route)  6.52 us
    convert_element_type x3, other arithmetic, merge_pair(): return (combined * (1.0 / math.sqrt(2.0))).astype(jnp.bfloat16)  6.07 us
    select_n x3, other arithmetic, on_device(): upper_image = jnp.where(upper_side, images, partner)  5.17 us
    another operation x1, loops' own time, prefix(): return lax.fori_loop(0, count - 1, lap, total)  4.51 us
    dynamic_slice x7, local copies, waits for them, and re-layouts, lap(): longer = join(total, pieces[position])  4.47 us
  transfers between devices with their start and end apart: 4, of which 4 were waited for; matrix products, arithmetic and copies ran while one was open for 0% of the time, Pallas kernels for 0%

commit v1 on v0

v1 whole, which is shorter than its diff:
```python
import functools
import math

import jax
import jax.numpy as jnp
from jax import lax
from jax.experimental import pallas as pl
from jax.experimental.pallas import tpu as pltpu
from jax.sharding import PartitionSpec as P

SECTIONS = 3
HALO = 72
CHUNK = 32
MESH = pl.DeviceIdType.MESH
F32 = jnp.float32
BF16 = jnp.bfloat16


def cos_sin_cycles(cycles):
    angle = (2.0 * math.pi) * (cycles - jnp.floor(cycles + 0.5))
    return jnp.cos(angle), jnp.sin(angle)


def cubic_weights(fractions):
    square = fractions * fractions
    cubed = square * fractions
    return (
        -0.5 * cubed + square - 0.5 * fractions,
        1.5 * cubed - 2.5 * square + 1.0,
        -1.5 * cubed + 2.0 * square + 0.5 * fractions,
        0.5 * cubed - 0.5 * square,
    )


def build_filter(replica_ref, filter_ref, segment):
    taps = replica_ref.shape[1]
    window = segment + taps
    row = lax.broadcasted_iota(jnp.int32, (16, window), 0)
    for part in range(2):
        response = replica_ref[part : part + 1, :].astype(F32)
        line = jnp.concatenate([response, jnp.zeros((1, segment), F32)], axis=1)
        base = jnp.broadcast_to(line, (16, window))
        for bit in range(4):
            base = jnp.where((row >> bit) & 1 == 1, pltpu.roll(base, 1 << bit, 1), base)
        for group in range(segment // 16):
            band = base if group == 0 else pltpu.roll(base, 16 * group, 1)
            band_up = band.astype(BF16)
            band_neg = (-band).astype(BF16)
            rows = slice(16 * group, 16 * group + 16)
            rows_low = slice(segment + 16 * group, segment + 16 * group + 16)
            for j in range(window // segment):
                piece = slice(j * segment, (j + 1) * segment)
                re_at = slice(2 * j * segment, (2 * j + 1) * segment)
                im_at = slice((2 * j + 1) * segment, (2 * j + 2) * segment)
                if part == 0:
                    filter_ref[rows, re_at] = band_up[:, piece]
                    filter_ref[rows_low, im_at] = band_up[:, piece]
                else:
                    filter_ref[rows, im_at] = band_up[:, piece]
                    filter_ref[rows_low, re_at] = band_neg[:, piece]


def kernel(
    owners,
    pulses,
    ingest_ref,
    replica_ref,
    counts_ref,
    track_ref,
    deviation_ref,
    shift_ref,
    offsets_ref,
    fraction_ref,
    out_ref,
    count_mine,
    count_all,
    filter_ref,
    stacked_ref,
    comp_ref,
    excess_ref,
    hand_ref,
    acc_ref,
    image_ref,
    other_ref,
    wide_ref,
    count_send,
    count_recv,
    hand_send,
    hand_recv,
    pair_send,
    pair_recv,
    merge_send,
    merge_recv,
):
    slots, blocks, both = ingest_ref.shape
    segment = both // 2
    moved = pulses - 1
    me = lax.axis_index("sub")
    sector = lax.axis_index("sector")

    def peer(step):
        return lax.rem(me + step, owners)

    barrier = pltpu.get_barrier_semaphore()

    def greet(step, carry):
        pl.semaphore_signal(barrier, inc=1, device_id={"sub": peer(step)}, device_id_type=MESH)
        return carry

    lax.fori_loop(1, owners, greet, 0)
    pl.semaphore_signal(barrier, inc=1, device_id={"sector": 1 - sector}, device_id_type=MESH)
    count_mine[...] = jnp.zeros(count_mine.shape, jnp.int32) + counts_ref[0]
    build_filter(replica_ref, filter_ref, segment)
    pl.semaphore_wait(barrier, owners)

    def count_copy(step, source):
        return pltpu.make_async_remote_copy(
            src_ref=count_mine,
            dst_ref=count_all.at[source],
            send_sem=count_send.at[step],
            recv_sem=count_recv.at[source],
            device_id={"sub": peer(step)},
            device_id_type=MESH,
        )

    def send_count(step, carry):
        count_copy(step, me).start()
        return carry

    lax.fori_loop(1, owners, send_count, 0)

    for slot in range(slots):
        rows = slice(slot * blocks, (slot + 1) * blocks)
        data = ingest_ref[slot]
        stacked_ref[rows, 0:both] = data
        wide = data.astype(F32)
        at = lax.broadcasted_iota(jnp.int32, wide.shape, 0)
        for j in range(1, stacked_ref.shape[1] // both):
            later = jnp.where(at < blocks - j, pltpu.roll(wide, blocks - j, 0), 0.0)
            stacked_ref[rows, j * both : (j + 1) * both] = later.astype(BF16)

    def compress(slot, carry):
        rows = pl.ds(pl.multiple_of(slot * blocks, blocks), blocks)
        comp_ref[slot] = lax.dot_general(
            filter_ref[...],
            stacked_ref[rows, :],
            (((1,), (1,)), ((), ())),
            preferred_element_type=F32,
        ).astype(BF16)
        return carry

    lax.fori_loop(0, slots, compress, 0)

    def wait_count(step, carry):
        count_copy(step, peer(step)).wait_recv()
        return carry

    lax.fori_loop(1, owners, wait_count, 0)
    count_all[me] = count_mine[...]

    def add_count(source, total):
        return total + jnp.where(source < me, count_all[source], 0)

    starts = lax.fori_loop(0, owners, add_count, jnp.zeros((8, 128), jnp.int32))
    track = track_ref[...]
    place = starts[0:1, 0:1] - me * pulses + track

    def chosen(target):
        return jnp.where((place == target) & (track >= 0), 1.0, 0.0).astype(F32)

    picks = [chosen(pulses + q) for q in range(moved)]
    pick_at = [
        [jnp.broadcast_to(picks[q][:, s : s + 1], (16, blocks)) for s in range(slots)]
        for q in range(moved)
    ]
    part_row = sector * segment

    def pick_rows(step, carry):
        at = pl.ds(pl.multiple_of(part_row + step * 16, 16), 16)
        to = pl.ds(pl.multiple_of(step * 16, 16), 16)
        values = [comp_ref[s, at, :].astype(F32) for s in range(slots)]
        for q in range(moved):
            total = pick_at[q][0] * values[0]
            for s in range(1, slots):
                total = total + pick_at[q][s] * values[s]
            excess_ref[q, to, :] = total.astype(BF16)
        return carry

    lax.fori_loop(0, segment // 16, pick_rows, 0)

    def hand_copy(q):
        return pltpu.make_async_remote_copy(
            src_ref=excess_ref.at[q],
            dst_ref=hand_ref.at[q, sector],
            send_sem=hand_send.at[q],
            recv_sem=hand_recv.at[q],
            device_id={"sub": peer(1)},
            device_id_type=MESH,
        )

    def pair_copy(q, part):
        return pltpu.make_async_remote_copy(
            src_ref=hand_ref.at[q, part],
            dst_ref=hand_ref.at[q, part],
            send_sem=pair_send.at[q],
            recv_sem=pair_recv.at[q],
            device_id={"sector": 1 - sector},
            device_id_type=MESH,
        )

    for q in range(moved):
        hand_copy(q).start()

    beams = pulses
    beam_index = lax.broadcasted_iota(jnp.int32, (beams, 1), 0) + sector * beams
    beam_angle = (beam_index.astype(F32) + 0.5) / (2.0 * beams) - 0.5
    pulse_index = lax.broadcasted_iota(jnp.int32, (1, pulses), 1).astype(F32)
    position = 2.0 * (pulse_index - (pulses - 1) / 2.0) + deviation_ref[...]
    cosine, sine = cos_sin_cycles(position * beam_angle)
    scale = 1.0 / math.sqrt(pulses)
    weight_re = (cosine * scale).astype(BF16).astype(F32)
    weight_im = (sine * scale).astype(BF16).astype(F32)
    slot_re = jnp.zeros((beams, slots), F32)
    slot_im = jnp.zeros((beams, slots), F32)
    for p in range(pulses):
        select = chosen(p)
        slot_re = slot_re + weight_re[:, p : p + 1] * select
        slot_im = slot_im + weight_im[:, p : p + 1] * select

    def spread(values, b, s, rows):
        return jnp.broadcast_to(values[b : b + 1, s : s + 1], (rows, blocks))

    for b in range(beams):
        own_re = [spread(slot_re, b, s, 16) for s in range(slots)]
        own_im = [spread(slot_im, b, s, 16) for s in range(slots)]

        def own_rows(step, carry):
            at = pl.ds(pl.multiple_of(step * 16, 16), 16)
            at_im = pl.ds(pl.multiple_of(segment + step * 16, 16), 16)
            total_re = jnp.zeros((16, blocks), F32)
            total_im = jnp.zeros((16, blocks), F32)
            for s in range(slots):
                real = comp_ref[s, at, :].astype(F32)
                imag = comp_ref[s, at_im, :].astype(F32)
                total_re = total_re + (own_re[s] * real - own_im[s] * imag)
                total_im = total_im + (own_im[s] * real + own_re[s] * imag)
            acc_ref[b, 0, at, :] = total_re
            acc_ref[b, 1, at, :] = total_im
            return carry

        lax.fori_loop(0, segment // 16, own_rows, 0)

    def section_terms(s):
        upper = (me >> s) & 1
        found = []
        for c in range(2):
            f = fraction_ref[s, c]
            o = offsets_ref[s, c]
            turn = lax.rem(17 * (o + 100), 20).astype(F32) * 0.05
            cosine, sine = cos_sin_cycles(turn + 0.85 * f)
            found.append(list(cubic_weights(f)) + [cosine * math.sqrt(0.5), sine * math.sqrt(0.5)])
        is_upper = jnp.zeros(fraction_ref.shape[2:], jnp.int32) + upper == 1
        own = [jnp.where(is_upper, u, l) for l, u in zip(*found)]
        far = [jnp.where(is_upper, l, u) for l, u in zip(*found)]
        return own, far

    terms = [section_terms(s) for s in range(SECTIONS)]

    def merge_copy(s, b):
        return pltpu.make_async_remote_copy(
            src_ref=image_ref.at[s, b],
            dst_ref=other_ref.at[s, b],
            send_sem=merge_send.at[s, b],
            recv_sem=merge_recv.at[s, b],
            device_id={"sub": me ^ (1 << s)},
            device_id_type=MESH,
        )

    lane = lax.broadcasted_iota(jnp.int32, (HALO, blocks), 1)

    def widen(source):
        for part in range(2):
            value = source[part].astype(F32)
            wide_ref[part, HALO : HALO + segment, :] = value
            wide_ref[part, 0:HALO, :] = jnp.where(
                lane > 0, pltpu.roll(value[segment - HALO :], 1, 1), 0.0
            )
            wide_ref[part, HALO + segment :, :] = jnp.where(
                lane < blocks - 1, pltpu.roll(value[:HALO], blocks - 1, 1), 0.0
            )

    def interpolate(s, b, far, store):
        upper = (me >> s) & 1
        child = 1 - upper if far else upper
        first = shift_ref[s, child, 0, b] + (HALO - 1)
        w0, w1, w2, w3, cosine, sine = [
            jnp.broadcast_to(t[:, b : b + 1], (CHUNK, blocks)) for t in terms[s][int(far)]
        ]

        def rows(step, carry):
            start = first + step * CHUNK
            sums = []
            for part in range(2):
                taps = [wide_ref[part, pl.ds(start + t, CHUNK), :] for t in range(4)]
                sums.append(w0 * taps[0] + w1 * taps[1] + w2 * taps[2] + w3 * taps[3])
            at = pl.ds(pl.multiple_of(step * CHUNK, CHUNK), CHUNK)
            store(at, 0, cosine * sums[0] - sine * sums[1])
            store(at, 1, sine * sums[0] + cosine * sums[1])
            return carry

        lax.fori_loop(0, segment // CHUNK, rows, 0)

    def own_side(s, b):
        widen(image_ref.at[s, b])

        def store(at, part, value):
            acc_ref[b, part, at, :] = value

        interpolate(s, b, False, store)

    def far_side(s, b):
        merge_copy(s, b).wait_recv()
        widen(other_ref.at[s, b])
        if s + 1 < SECTIONS:

            def store(at, part, value):
                image_ref[s + 1, b, part, at, :] = (acc_ref[b, part, at, :] + value).astype(BF16)

            interpolate(s, b, True, store)
            merge_copy(s + 1, b).start()
            own_side(s + 1, b)
        else:

            def store(at, part, value):
                acc_ref[b, part, at, :] = acc_ref[b, part, at, :] + value

            interpolate(s, b, True, store)
            for part in range(2):
                out_ref[part, b] = jnp.transpose(acc_ref[b, part]).astype(BF16)

    for q in range(moved):
        hand_copy(q).wait_recv()
        pair_copy(q, sector).start()
    for q in range(moved):
        pair_copy(q, 1 - sector).wait_recv()

    for b in range(beams):
        far_re = [spread(weight_re, b, q, 16) for q in range(moved)]
        far_im = [spread(weight_im, b, q, 16) for q in range(moved)]

        def first_rows(step, carry):
            at = pl.ds(pl.multiple_of(step * 16, 16), 16)
            total_re = acc_ref[b, 0, at, :]
            total_im = acc_ref[b, 1, at, :]
            for q in range(moved):
                real = hand_ref[q, 0, at, :].astype(F32)
                imag = hand_ref[q, 1, at, :].astype(F32)
                total_re = total_re + (far_re[q] * real - far_im[q] * imag)
                total_im = total_im + (far_im[q] * real + far_re[q] * imag)
            image_ref[0, b, 0, at, :] = total_re.astype(BF16)
            image_ref[0, b, 1, at, :] = total_im.astype(BF16)
            return carry

        lax.fori_loop(0, segment // 16, first_rows, 0)
        merge_copy(0, b).start()
    for b in range(beams):
        own_side(0, b)
    for wave in range(beams + SECTIONS - 1):
        for s in range(SECTIONS - 1, -1, -1):
            if 0 <= wave - s < beams:
                far_side(s, wave - s)

    def end_count(step, carry):
        count_copy(step, me).wait_send()
        return carry

    lax.fori_loop(1, owners, end_count, 0)
    for q in range(moved):
        hand_copy(q).wait_send()
        pair_copy(q, sector).wait_send()
    for s in range(SECTIONS):
        for b in range(beams):
            merge_copy(s, b).wait_send()


def on_device(owners, ingest, replica, counts, track_list, deviation, offsets, fraction):
    slots, blocks, both = ingest.shape
    pulses = slots // 2
    segment = both // 2
    taps = replica.shape[1]
    depth = (segment + taps) // segment
    moved = pulses - 1
    vmem = pl.BlockSpec(memory_space=pltpu.VMEM)
    smem = pl.BlockSpec(memory_space=pltpu.SMEM)
    dma = pltpu.SemaphoreType.DMA
    result = pl.pallas_call(
        functools.partial(kernel, owners, pulses),
        out_shape=jax.ShapeDtypeStruct((2, pulses, blocks, segment), BF16),
        in_specs=[vmem, vmem, smem, vmem, vmem, smem, vmem, vmem],
        out_specs=vmem,
        scratch_shapes=[
            pltpu.VMEM((8, 128), jnp.int32),
            pltpu.VMEM((owners, 8, 128), jnp.int32),
            pltpu.VMEM((both, depth * both), BF16),
            pltpu.VMEM((slots * blocks, depth * both), BF16),
            pltpu.VMEM((slots, both, blocks), BF16),
            pltpu.VMEM((moved, segment, blocks), BF16),
            pltpu.VMEM((moved, 2, segment, blocks), BF16),
            pltpu.VMEM((pulses, 2, segment, blocks), F32),
            pltpu.VMEM((SECTIONS, pulses, 2, segment, blocks), BF16),
            pltpu.VMEM((SECTIONS, pulses, 2, segment, blocks), BF16),
            pltpu.VMEM((2, segment + 2 * HALO, blocks), F32),
            dma((owners,)),
            dma((owners,)),
            dma((moved,)),
            dma((moved,)),
            dma((moved,)),
            dma((moved,)),
            dma((SECTIONS, pulses)),
            dma((SECTIONS, pulses)),
        ],
        compiler_params=pltpu.CompilerParams(
            collective_id=0, has_side_effects=True, vmem_limit_bytes=40 * 1024 * 1024
        ),
    )(
        ingest,
        replica,
        counts,
        track_list.reshape(1, slots),
        deviation.reshape(1, pulses),
        offsets,
        offsets,
        fraction,
    )
    return result.reshape(2, 1, pulses, blocks * segment)


def solution(mesh):
    return jax.shard_map(
        functools.partial(on_device, mesh.shape["sub"]),
        mesh=mesh,
        in_specs=(
            P(("groups", "sub"), None, None),
            P(),
            P(("groups", "sub")),
            P(("groups", "sub")),
            P(("groups", "sub")),
            P(None, None, ("groups", "sub"), "sector"),
            P(None, None, ("groups", "sub"), "sector"),
        ),
        out_specs=P(None, ("groups", "sub"), "sector", None),
        check_vma=False,
    )
```

time: 128 us -> 64.7 us (0.51)
  Pallas kernels: 0 us -> 59.3 us
  waiting for transfers between devices: 42.7 us -> 0 us
  other arithmetic: 18.7 us -> 0 us
  local copies, waits for them, and re-layouts: 21.9 us -> 4.4 us
  matrix products: 15 us -> 0 us
  blocking collectives: 13.1 us -> 0 us
  starting transfers between devices: 10.1 us -> 0 us
  loops' own time: 4.51 us -> 0 us
    pallas_call x0 -> x1, Pallas kernels: none -> 59.3 us  [on_device(): pl.pallas_call(functools.partial(kernel, owners, pulses), out_shape=jax.S...]
    ppermute x4 -> x0, waiting for transfers between devices: 42.7 us -> none  [the longest x3 34.5 us: partner_2(): return lax.ppermute(block, axis, route)]
    dot_general x16 -> x0, matrix products: 15 us -> none  [the longest x6 4.23 us: interpolate(): jnp.einsum('pbkj,bjn->pbkn', window, band_low, preferred_element_type=jnp...]
    unnamed x1 -> x0, blocking collectives: 13.1 us -> none
    ppermute x4 -> x0, starting transfers between devices: 10.1 us -> none  [the longest x3 6.52 us: partner_2(): return lax.ppermute(block, axis, route)]
    slice x28 -> x0, local copies, waits for them, and re-layouts: 7.37 us -> none  [the longest x6 1.95 us: interpolate(): padded[:, :, 0:blocks]]
    convert_element_type x4 -> x0, other arithmetic: 6.18 us -> none  [the longest x3 6.07 us: merge_pair(): return (combined * (1.0 / math.sqrt(2.0))).astype(jnp.bfloat16)]
    select_n x3 -> x0, other arithmetic: 5.17 us -> none  [on_device(): upper_image = jnp.where(upper_side, images, partner)]
  transfers between devices with their start and end apart: 4 -> 0, of which waited for: 4 -> 0; matrix products, arithmetic and copies ran while one was open for 0% -> 0% of each run, Pallas kernels for 0% -> 0%
where the time goes in v1:
time: 64.7 us; the launch traced here: 64.4 us
  Pallas kernels  59.3 us (92%)
  local copies, waits for them, and re-layouts  4.4 us (7%)
  between operations  0.7 us (1%)
    pallas_call x1, Pallas kernels, on_device(): pl.pallas_call(functools.partial(kernel, owners, pulses), out_shape=jax.S...  59.3 us
    unnamed x12, local copies, waits for them, and re-layouts  3.23 us

profile of v1, /device:TPU:0, one launch (start us, length us, event | category | flops | bytes accessed | tf_op | source)
XLA Modules:
  0.0 64.4 jit_solution(17491362911886311057)
XLA Ops:
  0.0 0.0 copy-start.1
  0.7 0.0 copy-start.3
  0.7 0.0 copy-start.4
  0.7 0.0 copy-done.1
  0.7 0.7 %copy-done.3 = bf16[2,512]{1,0:T(2,128)(2,1)S(1)} copy-done((bf16[2,512]{1,0:T(2,128)(2,1)S(1)}, bf16[2,512]{1,0:T(2,128)(2,1)}, u32[]{:S(2)}) %copy-start.3) | copy-done | bytes 2072
  1.4 0.0 copy-done.4
  1.4 0.0 copy-start
  1.4 1.2 %copy-done = bf16[8,128,512]{2,1,0:T(8,128)(2,1)S(1)} copy-done((bf16[8,128,512]{2,1,0:T(8,128)(2,1)S(1)}, bf16[8,128,512]{2,1,0:T(8,128)(2,1)}, u32[]{:S(2)}) %copy-start) | copy-done | bytes 1048600
  2.6 0.0 copy-start.2
  2.6 0.7 %copy-done.2 = f32[3,2,1,4]{3,2,1,0:T(1,128)S(1)} copy-done((f32[3,2,1,4]{3,2,1,0:T(1,128)S(1)}, f32[3,2,1,4]{3,2,1,0:T(1,128)}, u32[]{:S(2)}) %copy-start.2) | copy-done | bytes 120
  3.3 0.0 copy-start.5
  3.3 0.7 %copy-done.5 = f32[4]{0:T(128)S(1)} copy-done((f32[4]{0:T(128)S(1)}, f32[4]{0:T(128)}, u32[]{:S(2)}) %copy-start.5) | copy-done | bytes 40
  3.9 59.3 %shard_map.73 = bf16[2,4,128,256]{3,2,1,0:T(8,128)(2,1)S(1)} custom-call(bf16[8,128,512]{2,1,0:T(8,128)(2,1)S(1)} %copy-done, bf16[2,512]{1,0:T(2,128)(2,1)S(1)} %copy-done.3, s32[1]{0:T(128)S(6)} %copy.9.counts_ref, s32[1,8]{1,0:T(1,128)S(1)} %bitcast.5, f32[1,4]{1,0:T(1,128)S(1)} %bitcast.6, s32[3,2,1,4]{3,2,1,0:T(1,128)S(1)} %copy-done.1, ...), custom_call_target="tpu_custom_call" | custom-call | tf_op jit(solution)/shard_map/pallas_call | solution.py:396
  63.2 1.2 %reshape.11 = bf16[2,1,4,32768]{3,2,0,1:T(4,128)(2,1)} reshape(bf16[2,4,128,256]{3,2,1,0:T(8,128)(2,1)S(1)} %shard_map.73) | data formatting | bytes 1048576 | tf_op jit(solution)/shard_map/reshape | solution.py:435
Async XLA Ops:
  0.0 0.7 %copy-start.1 = (s32[3,2,1,4]{3,2,1,0:T(1,128)S(1)}, s32[3,2,1,4]{3,2,1,0:T(1,128)}, u32[]{:S(2)}) copy-start(s32[3,2,1,4]{3,2,1,0:T(1,128)} %offsets_ref.1) | copy-start | bytes 292
  0.7 0.7 %copy-start.3 = (bf16[2,512]{1,0:T(2,128)(2,1)S(1)}, bf16[2,512]{1,0:T(2,128)(2,1)}, u32[]{:S(2)}) copy-start(bf16[2,512]{1,0:T(2,128)(2,1)} %replica_ref.1) | copy-start | bytes 6148
  0.7 0.7 %copy-start.4 = (s32[8]{0:T(128)S(1)}, s32[8]{0:T(128)}, u32[]{:S(2)}) copy-start(s32[8]{0:T(128)} %param.10) | copy-start | bytes 100
  1.4 1.2 %copy-start = (bf16[8,128,512]{2,1,0:T(8,128)(2,1)S(1)}, bf16[8,128,512]{2,1,0:T(8,128)(2,1)}, u32[]{:S(2)}) copy-start(bf16[8,128,512]{2,1,0:T(8,128)(2,1)} %ingest_ref.1) | copy-start | bytes 3145732
  2.6 0.7 %copy-start.2 = (f32[3,2,1,4]{3,2,1,0:T(1,128)S(1)}, f32[3,2,1,4]{3,2,1,0:T(1,128)}, u32[]{:S(2)}) copy-start(f32[3,2,1,4]{3,2,1,0:T(1,128)} %fraction_ref.1) | copy-start | bytes 292
  3.3 0.7 %copy-start.5 = (f32[4]{0:T(128)S(1)}, f32[4]{0:T(128)}, u32[]{:S(2)}) copy-start(f32[4]{0:T(128)} %param.11) | copy-start | bytes 52

commit v2 on v1

--- a/solution.py
+++ b/solution.py
@@ -32,11 +32,11 @@
     )
 
 
-def build_filter(replica_ref, filter_ref, segment):
+def build_filter(replica_ref, filter_ref, segment, parts):
     taps = replica_ref.shape[1]
     window = segment + taps
     row = lax.broadcasted_iota(jnp.int32, (16, window), 0)
-    for part in range(2):
+    for part in parts:
         response = replica_ref[part : part + 1, :].astype(F32)
         line = jnp.concatenate([response, jnp.zeros((1, segment), F32)], axis=1)
         base = jnp.broadcast_to(line, (16, window))
@@ -63,6 +63,14 @@
 def kernel(
     owners,
     pulses,
+    ingest_hbm,
+    replica_hbm,
+    counts_hbm,
+    track_hbm,
+    deviation_hbm,
+    offsets_hbm,
+    fraction_hbm,
+    out_ref,
     ingest_ref,
     replica_ref,
     counts_ref,
@@ -71,7 +79,7 @@
     shift_ref,
     offsets_ref,
     fraction_ref,
-    out_ref,
+    load_sem,
     count_mine,
     count_all,
     filter_ref,
@@ -79,6 +87,7 @@
     comp_ref,
     excess_ref,
     hand_ref,
+    owned_ref,
     acc_ref,
     image_ref,
     other_ref,
@@ -109,8 +118,27 @@
 
     lax.fori_loop(1, owners, greet, 0)
     pl.semaphore_signal(barrier, inc=1, device_id={"sector": 1 - sector}, device_id_type=MESH)
+    loads = [
+        pltpu.make_async_copy(source, target, load_sem.at[i])
+        for i, (source, target) in enumerate(
+            [
+                (replica_hbm, replica_ref),
+                (counts_hbm, counts_ref),
+                (track_hbm, track_ref),
+                (deviation_hbm, deviation_ref),
+                (offsets_hbm, shift_ref),
+                (offsets_hbm, offsets_ref),
+                (fraction_hbm, fraction_ref),
+                (ingest_hbm, ingest_ref),
+            ]
+        )
+    ]
+    for load in loads:
+        load.start()
+    loads[0].wait()
+    build_filter(replica_ref, filter_ref, segment, [0])
+    loads[1].wait()
     count_mine[...] = jnp.zeros(count_mine.shape, jnp.int32) + counts_ref[0]
-    build_filter(replica_ref, filter_ref, segment)
     pl.semaphore_wait(barrier, owners)
 
     def count_copy(step, source):
@@ -129,9 +157,96 @@
 
     lax.fori_loop(1, owners, send_count, 0)
 
-    for slot in range(slots):
-        rows = slice(slot * blocks, (slot + 1) * blocks)
-        data = ingest_ref[slot]
+    build_filter(replica_ref, filter_ref, segment, [1])
+    for load in loads[2:]:
+        load.wait()
+
+    def wait_count(step, carry):
+        count_copy(step, peer(step)).wait_recv()
+        return carry
+
+    lax.fori_loop(1, owners, wait_count, 0)
+    count_all[me] = count_mine[...]
+
+    def add_count(source, total):
+        return total + jnp.where(source < me, count_all[source], 0)
+
+    starts = lax.fori_loop(0, owners, add_count, jnp.zeros((8, 128), jnp.int32))
+    track = track_ref[...]
+    place = starts[0:1, 0:1] - me * pulses + track
+
+    def chosen(target):
+        return jnp.where((place == target) & (track >= 0), 1.0, 0.0).astype(F32)
+
+    def pick_at(target):
+        pick = chosen(target)
+        return [
+            jnp.broadcast_to(pick[:, s : s + 1], (16, 128)).astype(BF16) for s in range(slots)
+        ]
+
+    def pick_piece(picks, at, lanes):
+        values = [ingest_ref[s, at, lanes] for s in range(slots)]
+        totals = []
+        for pick in picks:
+            total = pick[0] * values[0]
+            for s in range(1, slots):
+                total = total + pick[s] * values[s]
+            totals.append(total)
+        return totals
+
+    half = blocks // 2
+    pieces = [slice(128 * i, 128 * (i + 1)) for i in range(both // 128)]
+    excess_picks = [pick_at(pulses + q) for q in range(moved)]
+
+    def pick_rows(step, carry):
+        at = pl.ds(pl.multiple_of(sector * half + step * 16, 16), 16)
+        to = pl.ds(pl.multiple_of(step * 16, 16), 16)
+        for lanes in pieces:
+            for q, total in enumerate(pick_piece(excess_picks, at, lanes)):
+                excess_ref[q, to, lanes] = total
+        return carry
+
+    lax.fori_loop(0, half // 16, pick_rows, 0)
+
+    def half_of(part):
+        return pl.ds(pl.multiple_of(part * half, half), half)
+
+    def hand_copy(q):
+        return pltpu.make_async_remote_copy(
+            src_ref=excess_ref.at[q],
+            dst_ref=hand_ref.at[q, half_of(sector)],
+            send_sem=hand_send.at[q],
+            recv_sem=hand_recv.at[q],
+            device_id={"sub": peer(1)},
+            device_id_type=MESH,
+        )
+
+    def pair_copy(q, part):
+        return pltpu.make_async_remote_copy(
+            src_ref=hand_ref.at[q, half_of(part)],
+            dst_ref=hand_ref.at[q, half_of(part)],
+            send_sem=pair_send.at[q],
+            recv_sem=pair_recv.at[q],
+            device_id={"sector": 1 - sector},
+            device_id_type=MESH,
+        )
+
+    for q in range(moved):
+        hand_copy(q).start()
+
+    own_picks = [pick_at(p) for p in range(pulses)]
+
+    def own_pick_rows(step, carry):
+        at = pl.ds(pl.multiple_of(step * 16, 16), 16)
+        for lanes in pieces:
+            for p, total in enumerate(pick_piece(own_picks, at, lanes)):
+                owned_ref[p, at, lanes] = total
+        return carry
+
+    lax.fori_loop(0, blocks // 16, own_pick_rows, 0)
+
+    def stack(data, first):
+        rows = slice(first * blocks, (first + 1) * blocks)
         stacked_ref[rows, 0:both] = data
         wide = data.astype(F32)
         at = lax.broadcasted_iota(jnp.int32, wide.shape, 0)
@@ -139,77 +254,20 @@
             later = jnp.where(at < blocks - j, pltpu.roll(wide, blocks - j, 0), 0.0)
             stacked_ref[rows, j * both : (j + 1) * both] = later.astype(BF16)
 
-    def compress(slot, carry):
-        rows = pl.ds(pl.multiple_of(slot * blocks, blocks), blocks)
-        comp_ref[slot] = lax.dot_general(
+    def compress(first, many):
+        found = lax.dot_general(
             filter_ref[...],
-            stacked_ref[rows, :],
+            stacked_ref[first * blocks : (first + many) * blocks, :],
             (((1,), (1,)), ((), ())),
             preferred_element_type=F32,
         ).astype(BF16)
-        return carry
-
-    lax.fori_loop(0, slots, compress, 0)
-
-    def wait_count(step, carry):
-        count_copy(step, peer(step)).wait_recv()
-        return carry
-
-    lax.fori_loop(1, owners, wait_count, 0)
-    count_all[me] = count_mine[...]
-
-    def add_count(source, total):
-        return total + jnp.where(source < me, count_all[source], 0)
-
-    starts = lax.fori_loop(0, owners, add_count, jnp.zeros((8, 128), jnp.int32))
-    track = track_ref[...]
-    place = starts[0:1, 0:1] - me * pulses + track
-
-    def chosen(target):
-        return jnp.where((place == target) & (track >= 0), 1.0, 0.0).astype(F32)
-
-    picks = [chosen(pulses + q) for q in range(moved)]
-    pick_at = [
-        [jnp.broadcast_to(picks[q][:, s : s + 1], (16, blocks)) for s in range(slots)]
-        for q in range(moved)
-    ]
-    part_row = sector * segment
-
-    def pick_rows(step, carry):
-        at = pl.ds(pl.multiple_of(part_row + step * 16, 16), 16)
-        to = pl.ds(pl.multiple_of(step * 16, 16), 16)
-        values = [comp_ref[s, at, :].astype(F32) for s in range(slots)]
-        for q in range(moved):
-            total = pick_at[q][0] * values[0]
-            for s in range(1, slots):
-                total = total + pick_at[q][s] * values[s]
-            excess_ref[q, to, :] = total.astype(BF16)
-        return carry
-
-    lax.fori_loop(0, segment // 16, pick_rows, 0)
-
-    def hand_copy(q):
-        return pltpu.make_async_remote_copy(
-            src_ref=excess_ref.at[q],
-            dst_ref=hand_ref.at[q, sector],
-            send_sem=hand_send.at[q],
-            recv_sem=hand_recv.at[q],
-            device_id={"sub": peer(1)},
-            device_id_type=MESH,
-        )
-
-    def pair_copy(q, part):
-        return pltpu.make_async_remote_copy(
-            src_ref=hand_ref.at[q, part],
-            dst_ref=hand_ref.at[q, part],
-            send_sem=pair_send.at[q],
-            recv_sem=pair_recv.at[q],
-            device_id={"sector": 1 - sector},
-            device_id_type=MESH,
-        )
-
-    for q in range(moved):
-        hand_copy(q).start()
+        for i in range(many):
+            comp_ref[first + i] = found[:, i * blocks : (i + 1) * blocks]
+
+    for p in range(pulses):
+        stack(owned_ref[p], p)
+    for p in range(0, pulses, 2):
+        compress(p, 2)
 
     beams = pulses
     beam_index = lax.broadcasted_iota(jnp.int32, (beams, 1), 0) + sector * beams
@@ -220,26 +278,19 @@
     scale = 1.0 / math.sqrt(pulses)
     weight_re = (cosine * scale).astype(BF16).astype(F32)
     weight_im = (sine * scale).astype(BF16).astype(F32)
-    slot_re = jnp.zeros((beams, slots), F32)
-    slot_im = jnp.zeros((beams, slots), F32)
-    for p in range(pulses):
-        select = chosen(p)
-        slot_re = slot_re + weight_re[:, p : p + 1] * select
-        slot_im = slot_im + weight_im[:, p : p + 1] * select
-
     def spread(values, b, s, rows):
         return jnp.broadcast_to(values[b : b + 1, s : s + 1], (rows, blocks))
 
     for b in range(beams):
-        own_re = [spread(slot_re, b, s, 16) for s in range(slots)]
-        own_im = [spread(slot_im, b, s, 16) for s in range(slots)]
+        own_re = [spread(weight_re, b, s, 16) for s in range(pulses)]
+        own_im = [spread(weight_im, b, s, 16) for s in range(pulses)]
 
         def own_rows(step, carry):
             at = pl.ds(pl.multiple_of(step * 16, 16), 16)
             at_im = pl.ds(pl.multiple_of(segment + step * 16, 16), 16)
             total_re = jnp.zeros((16, blocks), F32)
             total_im = jnp.zeros((16, blocks), F32)
-            for s in range(slots):
+            for s in range(pulses):
                 real = comp_ref[s, at, :].astype(F32)
                 imag = comp_ref[s, at_im, :].astype(F32)
                 total_re = total_re + (own_re[s] * real - own_im[s] * imag)
@@ -343,6 +394,11 @@
         pair_copy(q, sector).start()
     for q in range(moved):
         pair_copy(q, 1 - sector).wait_recv()
+        stack(hand_ref[q], pulses + q)
+        if q % 2 == 1:
+            compress(pulses + q - 1, 2)
+        elif q == moved - 1:
+            compress(pulses + q, 1)
 
     for b in range(beams):
         far_re = [spread(weight_re, b, q, 16) for q in range(moved)]
@@ -350,11 +406,12 @@
 
         def first_rows(step, carry):
             at = pl.ds(pl.multiple_of(step * 16, 16), 16)
+            at_im = pl.ds(pl.multiple_of(segment + step * 16, 16), 16)
             total_re = acc_ref[b, 0, at, :]
             total_im = acc_ref[b, 1, at, :]
             for q in range(moved):
-                real = hand_ref[q, 0, at, :].astype(F32)
-                imag = hand_ref[q, 1, at, :].astype(F32)
+                real = comp_ref[pulses + q, at, :].astype(F32)
+                imag = comp_ref[pulses + q, at_im, :].astype(F32)
                 total_re = total_re + (far_re[q] * real - far_im[q] * imag)
                 total_im = total_im + (far_im[q] * real + far_re[q] * imag)
             image_ref[0, b, 0, at, :] = total_re.astype(BF16)
@@ -365,10 +422,12 @@
         merge_copy(0, b).start()
     for b in range(beams):
         own_side(0, b)
-    for wave in range(beams + SECTIONS - 1):
-        for s in range(SECTIONS - 1, -1, -1):
-            if 0 <= wave - s < beams:
-                far_side(s, wave - s)
+    order = sorted(
+        [(2 * s + b, -s, s, b) for s in range(SECTIONS - 1) for b in range(beams)]
+        + [(4 * SECTIONS + b, 0, SECTIONS - 1, b) for b in range(beams)]
+    )
+    for _, _, s, b in order:
+        far_side(s, b)
 
     def end_count(step, carry):
         count_copy(step, me).wait_send()
@@ -391,21 +450,31 @@
     depth = (segment + taps) // segment
     moved = pulses - 1
     vmem = pl.BlockSpec(memory_space=pltpu.VMEM)
-    smem = pl.BlockSpec(memory_space=pltpu.SMEM)
+    hbm = pl.BlockSpec(memory_space=pl.ANY)
     dma = pltpu.SemaphoreType.DMA
     result = pl.pallas_call(
         functools.partial(kernel, owners, pulses),
         out_shape=jax.ShapeDtypeStruct((2, pulses, blocks, segment), BF16),
-        in_specs=[vmem, vmem, smem, vmem, vmem, smem, vmem, vmem],
+        in_specs=[hbm] * 7,
         out_specs=vmem,
         scratch_shapes=[
+            pltpu.VMEM(ingest.shape, BF16),
+            pltpu.VMEM(replica.shape, BF16),
+            pltpu.SMEM(counts.shape, jnp.int32),
+            pltpu.VMEM((1, slots), jnp.int32),
+            pltpu.VMEM((1, pulses), F32),
+            pltpu.SMEM(offsets.shape, jnp.int32),
+            pltpu.VMEM(offsets.shape, jnp.int32),
+            pltpu.VMEM(fraction.shape, F32),
+            dma((8,)),
             pltpu.VMEM((8, 128), jnp.int32),
             pltpu.VMEM((owners, 8, 128), jnp.int32),
             pltpu.VMEM((both, depth * both), BF16),
-            pltpu.VMEM((slots * blocks, depth * both), BF16),
-            pltpu.VMEM((slots, both, blocks), BF16),
-            pltpu.VMEM((moved, segment, blocks), BF16),
-            pltpu.VMEM((moved, 2, segment, blocks), BF16),
+            pltpu.VMEM(((pulses + moved) * blocks, depth * both), BF16),
+            pltpu.VMEM((pulses + moved, both, blocks), BF16),
+            pltpu.VMEM((moved, blocks // 2, both), BF16),
+            pltpu.VMEM((moved, blocks, both), BF16),
+            pltpu.VMEM((pulses, blocks, both), BF16),
             pltpu.VMEM((pulses, 2, segment, blocks), F32),
             pltpu.VMEM((SECTIONS, pulses, 2, segment, blocks), BF16),
             pltpu.VMEM((SECTIONS, pulses, 2, segment, blocks), BF16),
@@ -429,7 +498,6 @@
         track_list.reshape(1, slots),
         deviation.reshape(1, pulses),
         offsets,
-        offsets,
         fraction,
     )
     return result.reshape(2, 1, pulses, blocks * segment)

time: 64.7 us -> 57.6 us (0.89)
  Pallas kernels: 59.3 us -> 52.2 us
    pallas_call x1, Pallas kernels: 59.3 us -> 52.2 us  [on_device(): pl.pallas_call(functools.partial(kernel, owners, pulses), out_shape=jax.S...]
where the time goes in v2:
time: 57.6 us; the launch traced here: 57.3 us
  Pallas kernels  52.2 us (91%)
  local copies, waits for them, and re-layouts  4.4 us (8%)
  between operations  0.7 us (1%)
    pallas_call x1, Pallas kernels, on_device(): pl.pallas_call(functools.partial(kernel, owners, pulses), out_shape=jax.S...  52.2 us
    unnamed x12, local copies, waits for them, and re-layouts  3.23 us
    reshape x1, local copies, waits for them, and re-layouts, on_device(): return result.reshape(2, 1, pulses, blocks * segment)  1.17 us

profile of v2, /device:TPU:0, one launch (start us, length us, event | category | flops | bytes accessed | tf_op | source)
XLA Modules:
  0.0 57.3 jit_solution(11907144126657395597)
XLA Ops:
  0.0 0.0 copy-start.1
  0.7 0.0 copy-start.3
  0.7 0.0 copy-start.4
  0.7 0.0 copy-done.1
  0.7 0.7 %copy-done.3 = bf16[2,512]{1,0:T(2,128)(2,1)S(1)} copy-done((bf16[2,512]{1,0:T(2,128)(2,1)S(1)}, bf16[2,512]{1,0:T(2,128)(2,1)}, u32[]{:S(2)}) %copy-start.3) | copy-done | bytes 2072
  1.4 0.0 copy-done.4
  1.4 0.0 copy-start
  1.4 1.2 %copy-done = bf16[8,128,512]{2,1,0:T(8,128)(2,1)S(1)} copy-done((bf16[8,128,512]{2,1,0:T(8,128)(2,1)S(1)}, bf16[8,128,512]{2,1,0:T(8,128)(2,1)}, u32[]{:S(2)}) %copy-start) | copy-done | bytes 1048600
  2.6 0.0 copy-start.2
  2.6 0.7 %copy-done.2 = f32[3,2,1,4]{3,2,1,0:T(1,128)S(1)} copy-done((f32[3,2,1,4]{3,2,1,0:T(1,128)S(1)}, f32[3,2,1,4]{3,2,1,0:T(1,128)}, u32[]{:S(2)}) %copy-start.2) | copy-done | bytes 120
  3.3 0.0 copy-start.5
  3.3 0.7 %copy-done.5 = f32[4]{0:T(128)S(1)} copy-done((f32[4]{0:T(128)S(1)}, f32[4]{0:T(128)}, u32[]{:S(2)}) %copy-start.5) | copy-done | bytes 40
  3.9 52.2 %shard_map.73 = bf16[2,4,128,256]{3,2,1,0:T(8,128)(2,1)S(1)} custom-call(bf16[8,128,512]{2,1,0:T(8,128)(2,1)S(1)} %copy-done, bf16[2,512]{1,0:T(2,128)(2,1)S(1)} %copy-done.3, s32[1]{0:T(128)S(6)} %copy.9.counts_hbm, s32[1,8]{1,0:T(1,128)S(1)} %bitcast.5, f32[1,4]{1,0:T(1,128)S(1)} %bitcast.6, s32[3,2,1,4]{3,2,1,0:T(1,128)S(1)} %copy-done.1, ...), custom_call_target="tpu_custom_call" | custom-call | tf_op jit(solution)/shard_map/pallas_call | solution.py:455
  56.1 1.2 %reshape.11 = bf16[2,1,4,32768]{3,2,0,1:T(4,128)(2,1)} reshape(bf16[2,4,128,256]{3,2,1,0:T(8,128)(2,1)S(1)} %shard_map.73) | data formatting | bytes 1048576 | tf_op jit(solution)/shard_map/reshape | solution.py:503
Async XLA Ops:
  0.0 0.7 %copy-start.1 = (s32[3,2,1,4]{3,2,1,0:T(1,128)S(1)}, s32[3,2,1,4]{3,2,1,0:T(1,128)}, u32[]{:S(2)}) copy-start(s32[3,2,1,4]{3,2,1,0:T(1,128)} %offsets_hbm.1) | copy-start | bytes 292
  0.7 0.7 %copy-start.3 = (bf16[2,512]{1,0:T(2,128)(2,1)S(1)}, bf16[2,512]{1,0:T(2,128)(2,1)}, u32[]{:S(2)}) copy-start(bf16[2,512]{1,0:T(2,128)(2,1)} %replica_hbm.1) | copy-start | bytes 6148
  0.7 0.7 %copy-start.4 = (s32[8]{0:T(128)S(1)}, s32[8]{0:T(128)}, u32[]{:S(2)}) copy-start(s32[8]{0:T(128)} %param.10) | copy-start | bytes 100
  1.4 1.2 %copy-start = (bf16[8,128,512]{2,1,0:T(8,128)(2,1)S(1)}, bf16[8,128,512]{2,1,0:T(8,128)(2,1)}, u32[]{:S(2)}) copy-start(bf16[8,128,512]{2,1,0:T(8,128)(2,1)} %ingest_hbm.1) | copy-start | bytes 3145732
  2.6 0.7 %copy-start.2 = (f32[3,2,1,4]{3,2,1,0:T(1,128)S(1)}, f32[3,2,1,4]{3,2,1,0:T(1,128)}, u32[]{:S(2)}) copy-start(f32[3,2,1,4]{3,2,1,0:T(1,128)} %fraction_hbm.1) | copy-start | bytes 292
  3.3 0.7 %copy-start.5 = (f32[4]{0:T(128)S(1)}, f32[4]{0:T(128)}, u32[]{:S(2)}) copy-start(f32[4]{0:T(128)} %param.11) | copy-start | bytes 52

commit v3 on v2

--- a/solution.py
+++ b/solution.py
@@ -87,7 +87,6 @@
     comp_ref,
     excess_ref,
     hand_ref,
-    owned_ref,
     acc_ref,
     image_ref,
     other_ref,
@@ -136,7 +135,36 @@
     for load in loads:
         load.start()
     loads[0].wait()
-    build_filter(replica_ref, filter_ref, segment, [0])
+    build_filter(replica_ref, filter_ref, segment, [0, 1])
+    loads[7].wait()
+
+    def stack(data, first):
+        rows = slice(first * blocks, (first + 1) * blocks)
+        stacked_ref[rows, 0:both] = data
+        wide = data.astype(F32)
+        at = lax.broadcasted_iota(jnp.int32, wide.shape, 0)
+        for j in range(1, stacked_ref.shape[1] // both):
+            later = jnp.where(at < blocks - j, pltpu.roll(wide, blocks - j, 0), 0.0)
+            stacked_ref[rows, j * both : (j + 1) * both] = later.astype(BF16)
+
+    def compress(first, many):
+        found = lax.dot_general(
+            filter_ref[...],
+            stacked_ref[first * blocks : (first + many) * blocks, :],
+            (((1,), (1,)), ((), ())),
+            preferred_element_type=F32,
+        ).astype(BF16)
+        for i in range(many):
+            comp_ref[first + i] = found[:, i * blocks : (i + 1) * blocks]
+
+    def compress_slots(first, many):
+        for slot in range(first, first + many):
+            stack(ingest_ref[slot], slot)
+        for slot in range(first, first + many, 2):
+            compress(slot, 2)
+
+    early = slots // 4 * 2
+    compress_slots(0, early)
     loads[1].wait()
     count_mine[...] = jnp.zeros(count_mine.shape, jnp.int32) + counts_ref[0]
     pl.semaphore_wait(barrier, owners)
@@ -157,8 +185,8 @@
 
     lax.fori_loop(1, owners, send_count, 0)
 
-    build_filter(replica_ref, filter_ref, segment, [1])
-    for load in loads[2:]:
+    compress_slots(early, slots - early)
+    for load in loads[2:7]:
         load.wait()
 
     def wait_count(step, carry):
@@ -181,40 +209,28 @@
     def pick_at(target):
         pick = chosen(target)
         return [
-            jnp.broadcast_to(pick[:, s : s + 1], (16, 128)).astype(BF16) for s in range(slots)
+            jnp.broadcast_to(pick[:, s : s + 1], (16, blocks)).astype(BF16) for s in range(slots)
         ]
 
-    def pick_piece(picks, at, lanes):
-        values = [ingest_ref[s, at, lanes] for s in range(slots)]
-        totals = []
-        for pick in picks:
+    excess_picks = [pick_at(pulses + q) for q in range(moved)]
+
+    def pick_rows(step, carry):
+        at = pl.ds(pl.multiple_of(sector * segment + step * 16, 16), 16)
+        to = pl.ds(pl.multiple_of(step * 16, 16), 16)
+        values = [comp_ref[s, at, :] for s in range(slots)]
+        for q, pick in enumerate(excess_picks):
             total = pick[0] * values[0]
             for s in range(1, slots):
                 total = total + pick[s] * values[s]
-            totals.append(total)
-        return totals
-
-    half = blocks // 2
-    pieces = [slice(128 * i, 128 * (i + 1)) for i in range(both // 128)]
-    excess_picks = [pick_at(pulses + q) for q in range(moved)]
-
-    def pick_rows(step, carry):
-        at = pl.ds(pl.multiple_of(sector * half + step * 16, 16), 16)
-        to = pl.ds(pl.multiple_of(step * 16, 16), 16)
-        for lanes in pieces:
-            for q, total in enumerate(pick_piece(excess_picks, at, lanes)):
-                excess_ref[q, to, lanes] = total
+            excess_ref[q, to, :] = total
         return carry
 
-    lax.fori_loop(0, half // 16, pick_rows, 0)
-
-    def half_of(part):
-        return pl.ds(pl.multiple_of(part * half, half), half)
+    lax.fori_loop(0, segment // 16, pick_rows, 0)
 
     def hand_copy(q):
         return pltpu.make_async_remote_copy(
             src_ref=excess_ref.at[q],
-            dst_ref=hand_ref.at[q, half_of(sector)],
+            dst_ref=hand_ref.at[q, sector],
             send_sem=hand_send.at[q],
             recv_sem=hand_recv.at[q],
             device_id={"sub": peer(1)},
@@ -223,51 +239,22 @@
 
     def pair_copy(q, part):
         return pltpu.make_async_remote_copy(
-            src_ref=hand_ref.at[q, half_of(part)],
-            dst_ref=hand_ref.at[q, half_of(part)],
+            src_ref=hand_ref.at[q, part],
+            dst_ref=hand_ref.at[q, part],
             send_sem=pair_send.at[q],
             recv_sem=pair_recv.at[q],
             device_id={"sector": 1 - sector},
             device_id_type=MESH,
         )
 
-    for q in range(moved):
-        hand_copy(q).start()
-
-    own_picks = [pick_at(p) for p in range(pulses)]
-
-    def own_pick_rows(step, carry):
-        at = pl.ds(pl.multiple_of(step * 16, 16), 16)
-        for lanes in pieces:
-            for p, total in enumerate(pick_piece(own_picks, at, lanes)):
-                owned_ref[p, at, lanes] = total
-        return carry
-
-    lax.fori_loop(0, blocks // 16, own_pick_rows, 0)
-
-    def stack(data, first):
-        rows = slice(first * blocks, (first + 1) * blocks)
-        stacked_ref[rows, 0:both] = data
-        wide = data.astype(F32)
-        at = lax.broadcasted_iota(jnp.int32, wide.shape, 0)
-        for j in range(1, stacked_ref.shape[1] // both):
-            later = jnp.where(at < blocks - j, pltpu.roll(wide, blocks - j, 0), 0.0)
-            stacked_ref[rows, j * both : (j + 1) * both] = later.astype(BF16)
-
-    def compress(first, many):
-        found = lax.dot_general(
-            filter_ref[...],
-            stacked_ref[first * blocks : (first + many) * blocks, :],
-            (((1,), (1,)), ((), ())),
-            preferred_element_type=F32,
-        ).astype(BF16)
-        for i in range(many):
-            comp_ref[first + i] = found[:, i * blocks : (i + 1) * blocks]
-
-    for p in range(pulses):
-        stack(owned_ref[p], p)
-    for p in range(0, pulses, 2):
-        compress(p, 2)
+    @pl.when(me < owners - 1)
+    def _():
+        for q in range(moved):
+            hand_copy(q).start()
+
+    @pl.when(me == 0)
+    def _():
+        hand_ref[...] = jnp.zeros(hand_ref.shape, BF16)
 
     beams = pulses
     beam_index = lax.broadcasted_iota(jnp.int32, (beams, 1), 0) + sector * beams
@@ -278,19 +265,26 @@
     scale = 1.0 / math.sqrt(pulses)
     weight_re = (cosine * scale).astype(BF16).astype(F32)
     weight_im = (sine * scale).astype(BF16).astype(F32)
+    slot_re = jnp.zeros((beams, slots), F32)
+    slot_im = jnp.zeros((beams, slots), F32)
+    for p in range(pulses):
+        select = chosen(p)
+        slot_re = slot_re + weight_re[:, p : p + 1] * select
+        slot_im = slot_im + weight_im[:, p : p + 1] * select
+
     def spread(values, b, s, rows):
         return jnp.broadcast_to(values[b : b + 1, s : s + 1], (rows, blocks))
 
     for b in range(beams):
-        own_re = [spread(weight_re, b, s, 16) for s in range(pulses)]
-        own_im = [spread(weight_im, b, s, 16) for s in range(pulses)]
+        own_re = [spread(slot_re, b, s, 16) for s in range(slots)]
+        own_im = [spread(slot_im, b, s, 16) for s in range(slots)]
 
         def own_rows(step, carry):
             at = pl.ds(pl.multiple_of(step * 16, 16), 16)
             at_im = pl.ds(pl.multiple_of(segment + step * 16, 16), 16)
             total_re = jnp.zeros((16, blocks), F32)
             total_im = jnp.zeros((16, blocks), F32)
-            for s in range(pulses):
+            for s in range(slots):
                 real = comp_ref[s, at, :].astype(F32)
                 imag = comp_ref[s, at_im, :].astype(F32)
                 total_re = total_re + (own_re[s] * real - own_im[s] * imag)
@@ -370,6 +364,9 @@
         interpolate(s, b, False, store)
 
     def far_side(s, b):
+        if s == 0 and b + 1 < beams:
+            merge_copy(0, b).wait_send()
+            merge_copy(0, b + 1).start()
         merge_copy(s, b).wait_recv()
         widen(other_ref.at[s, b])
         if s + 1 < SECTIONS:
@@ -389,16 +386,13 @@
             for part in range(2):
                 out_ref[part, b] = jnp.transpose(acc_ref[b, part]).astype(BF16)
 
-    for q in range(moved):
-        hand_copy(q).wait_recv()
-        pair_copy(q, sector).start()
-    for q in range(moved):
-        pair_copy(q, 1 - sector).wait_recv()
-        stack(hand_ref[q], pulses + q)
-        if q % 2 == 1:
-            compress(pulses + q - 1, 2)
-        elif q == moved - 1:
-            compress(pulses + q, 1)
+    @pl.when(me > 0)
+    def _():
+        for q in range(moved):
+            hand_copy(q).wait_recv()
+            pair_copy(q, sector).start()
+        for q in range(moved):
+            pair_copy(q, 1 - sector).wait_recv()
 
     for b in range(beams):
         far_re = [spread(weight_re, b, q, 16) for q in range(moved)]
@@ -406,12 +400,11 @@
 
         def first_rows(step, carry):
             at = pl.ds(pl.multiple_of(step * 16, 16), 16)
-            at_im = pl.ds(pl.multiple_of(segment + step * 16, 16), 16)
             total_re = acc_ref[b, 0, at, :]
             total_im = acc_ref[b, 1, at, :]
             for q in range(moved):
-                real = comp_ref[pulses + q, at, :].astype(F32)
-                imag = comp_ref[pulses + q, at_im, :].astype(F32)
+                real = hand_ref[q, 0, at, :].astype(F32)
+                imag = hand_ref[q, 1, at, :].astype(F32)
                 total_re = total_re + (far_re[q] * real - far_im[q] * imag)
                 total_im = total_im + (far_im[q] * real + far_re[q] * imag)
             image_ref[0, b, 0, at, :] = total_re.astype(BF16)
@@ -419,7 +412,8 @@
             return carry
 
         lax.fori_loop(0, segment // 16, first_rows, 0)
-        merge_copy(0, b).start()
+        if b == 0:
+            merge_copy(0, b).start()
     for b in range(beams):
         own_side(0, b)
     order = sorted(
@@ -434,12 +428,21 @@
         return carry
 
     lax.fori_loop(1, owners, end_count, 0)
-    for q in range(moved):
-        hand_copy(q).wait_send()
-        pair_copy(q, sector).wait_send()
+
+    @pl.when(me < owners - 1)
+    def _():
+        for q in range(moved):
+            hand_copy(q).wait_send()
+
+    @pl.when(me > 0)
+    def _():
+        for q in range(moved):
+            pair_copy(q, sector).wait_send()
+
     for s in range(SECTIONS):
         for b in range(beams):
-            merge_copy(s, b).wait_send()
+            if s > 0 or b == beams - 1:
+                merge_copy(s, b).wait_send()
 
 
 def on_device(owners, ingest, replica, counts, track_list, deviation, offsets, fraction):
@@ -470,11 +473,10 @@
             pltpu.VMEM((8, 128), jnp.int32),
             pltpu.VMEM((owners, 8, 128), jnp.int32),
             pltpu.VMEM((both, depth * both), BF16),
-            pltpu.VMEM(((pulses + moved) * blocks, depth * both), BF16),
-            pltpu.VMEM((pulses + moved, both, blocks), BF16),
-            pltpu.VMEM((moved, blocks // 2, both), BF16),
-            pltpu.VMEM((moved, blocks, both), BF16),
-            pltpu.VMEM((pulses, blocks, both), BF16),
+            pltpu.VMEM((slots * blocks, depth * both), BF16),
+            pltpu.VMEM((slots, both, blocks), BF16),
+            pltpu.VMEM((moved, segment, blocks), BF16),
+            pltpu.VMEM((moved, 2, segment, blocks), BF16),
             pltpu.VMEM((pulses, 2, segment, blocks), F32),
             pltpu.VMEM((SECTIONS, pulses, 2, segment, blocks), BF16),
             pltpu.VMEM((SECTIONS, pulses, 2, segment, blocks), BF16),
@@ -489,7 +491,7 @@
             dma((SECTIONS, pulses)),
         ],
         compiler_params=pltpu.CompilerParams(
-            collective_id=0, has_side_effects=True, vmem_limit_bytes=40 * 1024 * 1024
+            collective_id=0, has_side_effects=True, vmem_limit_bytes=60 * 1024 * 1024
         ),
     )(
         ingest,

time: 57.6 us -> 55.2 us (0.958)
  local copies, waits for them, and re-layouts: 4.4 us -> 2.23 us
    unnamed x12 -> x0, local copies, waits for them, and re-layouts: 3.23 us -> none
    reshape x1, local copies, waits for them, and re-layouts: 1.17 us -> 2.23 us  [on_device(): return result.reshape(2, 1, pulses, blocks * segment)]
where the time goes in v3:
time: 55.2 us; the launch traced here: 55 us
  Pallas kernels  52.2 us (95%)
  local copies, waits for them, and re-layouts  2.23 us (4%)
  between operations  0.66 us (1%)
    pallas_call x1, Pallas kernels, on_device(): pl.pallas_call(functools.partial(kernel, owners, pulses), out_shape=jax.S...  52.2 us
    reshape x1, local copies, waits for them, and re-layouts, on_device(): return result.reshape(2, 1, pulses, blocks * segment)  2.23 us

profile of v3, /device:TPU:0, one launch (start us, length us, event | category | flops | bytes accessed | tf_op | source)
XLA Modules:
  0.0 55.0 jit_solution(13105267470957023475)
XLA Ops:
  0.7 52.2 %shard_map.73 = bf16[2,4,128,256]{3,2,1,0:T(8,128)(2,1)} custom-call(bf16[8,128,512]{2,1,0:T(8,128)(2,1)} %ingest_hbm.1, bf16[2,512]{1,0:T(2,128)(2,1)} %replica_hbm.1, s32[1]{0:T(128)S(6)} %copy.9.counts_hbm, s32[1,8]{1,0:T(1,128)} %bitcast.5, f32[1,4]{1,0:T(1,128)} %bitcast.6, s32[3,2,1,4]{3,2,1,0:T(1,128)} %offsets_hbm.1, f32[3,2,1,4]{3,2,1,0:T(1,128)} %fraction_hbm.1), custom_call_target="tpu_custom_call" | custom-call | tf_op jit(solution)/shard_map/pallas_call | solution.py:458
  52.8 2.2 %reshape.11 = bf16[2,1,4,32768]{3,2,0,1:T(4,128)(2,1)} reshape(bf16[2,4,128,256]{3,2,1,0:T(8,128)(2,1)} %shard_map.73) | data formatting | bytes 1048576 | tf_op jit(solution)/shard_map/reshape | solution.py:505
